TPU v7x, 32 devices: a whole 2x2x4 slice. The times are simulated.
32 devices in a mesh: sph: 8 (over z, core), wave: 4 (over y, x).
Axes of the slice: x: 2, y: 2, z: 4, core: 2. Of those that a mesh axis runs over, the one named last changes fastest.
Arguments:
- coefficients: float32 [8, 96, 1024], P(None, None, 'sph'), may hold values from -6 to 6
- incident: float32 [8, 96, 1024], P(None, None, 'sph'), may hold values from -6 to 6
- positions: float32 [3, 1024], P(None, 'sph'), may hold values from 0 to 1
- neighbour_index: int32 [12, 1024], P(None, 'sph'), may hold values from 0 to 1023, as said below
- link_class: int32 [12, 1024], P(None, 'sph'), may hold values from 0 to 25
- link_count: int32 [1024], P('sph'), may hold values from 1 to 12, as said below
- sphere_type: int32 [1024], P('sph'), may hold values from 0 to 3
- translation: float32 [2, 26, 48, 48], replicated, may hold values from -0.1875 to 0.1875
- t_matrix: float32 [2, 4, 48, 48], replicated, may hold values from -0.375 to 0.375
- wave_grid: int32 [2, 2048], P(None, 'wave'), may hold values from -64 to 63
- vertical: float32 [2048], P('wave'), may hold values from 0.5 to 4
- expansion: float32 [2, 2, 48, 2048], P(None, None, None, 'wave'), may hold values from -0.01953125 to 0.01953125
- reflection: float32 [2, 2, 2, 2048], P(None, None, None, 'wave'), may hold values from -3 to 3
- projector: float32 [2, 48, 2, 2048], P(None, None, None, 'wave'), may hold values from -0.046875 to 0.046875
Outputs:
- updated: float32 [8, 96, 1024], P(None, None, 'sph')
Inputs may be any that keep to these rules, and one draw needn't show every extreme that they name: `neighbour_index`: every entry lies within 128 of its own sphere's index; slots at or past link_count hold valid indices that are not used. `link_count`: the spheres of some aligned blocks of 128 have many more live slots than others.
All inputs are finite; a program needn't handle non-finite values.
Results may differ from a plain program's by a relative error of at most 0.0003.
Values sent between devices are 32-bit elements; how exact they have to be, the bound alone decides.
A program may use at most 64 MiB of HBM per device.

v0:
```python
import functools
import math

import jax
import jax.numpy as jnp
from jax import lax
from jax.experimental import pallas as pl
from jax.experimental.pallas import tpu as pltpu
from jax.sharding import PartitionSpec as P

LANES = 128
MESH = pl.DeviceIdType.MESH
SIN_TERMS = [(-1) ** k * math.pi ** (2 * k + 1) / math.factorial(2 * k + 1) for k in range(6)]
COS_TERMS = [(-1) ** k * math.pi ** (2 * k) / math.factorial(2 * k) for k in range(7)]


def realify(complex_pair):
    upper_half = jnp.concatenate([complex_pair[0], -complex_pair[1]], axis=-1)
    lower_half = jnp.concatenate([complex_pair[1], complex_pair[0]], axis=-1)
    return jnp.concatenate([upper_half, lower_half], axis=-2)


def split(value):
    high = value.astype(jnp.bfloat16)
    return high, (value - high.astype(jnp.float32)).astype(jnp.bfloat16)


def dot(left, right):
    return jnp.dot(left, right, preferred_element_type=jnp.float32)


def dot3(left, right):
    return dot(left[0], right[0]) + (dot(left[0], right[1]) + dot(left[1], right[0]))


def horner(terms, x):
    total = jnp.full_like(x, terms[-1])
    for term in reversed(terms[:-1]):
        total = total * x + term
    return total


def cos_sin(turns):
    r = turns - jnp.floor(turns + 0.5)
    square = r * r
    s = r * horner(SIN_TERMS, square)
    c = horner(COS_TERMS, square)
    return 1.0 - 2.0 * (s * s), 2.0 * (s * c)


def kernel(
    n_sph, n_wave, offsets, types,
    coef_ref, inc_ref, pos_ref, index_ref, class_ref, count_ref, type_ref, op_ref, t_ref,
    grid_ref, vert_ref, exp_ref, refl_ref, proj_ref,
    out_ref,
    halo, part, part_in, spec, mirrored, up_high, up_low, picked, bin_high, bin_low, resp, resp_in,
    halo_send, halo_recv, part_send, part_recv, spec_send, spec_recv,
    resp_send, resp_recv, out_send, out_recv,
):
    me = lax.axis_index("sph")
    mine = lax.axis_index("wave")
    illums, rows, block = coef_ref.shape
    modes = rows // 2
    waves = vert_ref.shape[1]
    slots = index_ref.shape[0]
    own = illums // n_wave
    first = mine * own
    share = part.shape[1]

    barrier = pltpu.get_barrier_semaphore()
    for d in range(1, n_sph):
        pl.semaphore_signal(barrier, inc=1, device_id={"sph": lax.rem(me + d, n_sph)}, device_id_type=MESH)
    for d in range(1, n_wave):
        pl.semaphore_signal(barrier, inc=1, device_id={"wave": lax.rem(mine + d, n_wave)}, device_id_type=MESH)
    pl.semaphore_wait(barrier, n_sph + n_wave - 2)

    def halo_copy(side):
        step = 1 if side == 0 else n_sph - 1
        return pltpu.make_async_remote_copy(
            src_ref=coef_ref.at[pl.ds(first, own)],
            dst_ref=halo.at[side],
            send_sem=halo_send.at[side],
            recv_sem=halo_recv.at[side],
            device_id={"sph": lax.rem(me + step, n_sph)},
            device_id_type=MESH,
        )

    for side in range(2):
        halo_copy(side).start()

    def angles(w):
        wave = slice(w * LANES, (w + 1) * LANES)
        across = grid_ref[0:1, wave].astype(jnp.float32)
        along = grid_ref[1:2, wave].astype(jnp.float32)
        plane = pos_ref[:, 0:1] * across + pos_ref[:, 1:2] * along
        height = pos_ref[:, 2:3] * (vert_ref[:, wave] * (0.5 / math.pi))
        return plane - jnp.floor(plane + 0.5), height

    coef = split(coef_ref[...].reshape(illums * rows, block))
    for w in range(waves // LANES):
        wave = slice(w * LANES, (w + 1) * LANES)
        plane, height = angles(w)
        phases = split(jnp.concatenate(cos_sin(plane - height), axis=1))
        products = dot3(coef, phases)
        for b in range(illums):
            real = products[b * rows : b * rows + modes]
            imag = products[b * rows + modes : (b + 1) * rows]
            spec_real = real[:, :LANES] + imag[:, LANES:]
            spec_imag = imag[:, :LANES] - real[:, LANES:]
            for p in range(2):
                e_real, e_imag = exp_ref[0, p, :, wave], exp_ref[1, p, :, wave]
                sums = (e_real * spec_real - e_imag * spec_imag, e_real * spec_imag + e_imag * spec_real)
                for c in range(2):
                    row = b * 4 + c * 2 + p
                    part[row // share, row % share : row % share + 1, wave] = jnp.sum(
                        sums[c], axis=0, keepdims=True
                    )

    part_copies = []
    for d in range(1, n_sph):
        peer = lax.rem(me + d, n_sph)
        copy = pltpu.make_async_remote_copy(
            src_ref=part.at[peer],
            dst_ref=part_in.at[d],
            send_sem=part_send.at[d],
            recv_sem=part_recv.at[d],
            device_id={"sph": peer},
            device_id_type=MESH,
        )
        copy.start()
        part_copies.append(copy)

    for w in range(waves // LANES):
        wave = slice(w * LANES, (w + 1) * LANES)
        plane, height = angles(w)
        cos, sin = cos_sin(plane + height)
        high, low = split(jnp.concatenate([cos.T, sin.T], axis=1))
        up_high[wave, :] = high
        up_low[wave, :] = low

    total = part[me]
    for d, copy in enumerate(part_copies, 1):
        copy.wait_recv()
        total = total + part_in[d]
    spec[me] = total

    spec_copies = []
    for d in range(1, n_sph):
        copy = pltpu.make_async_remote_copy(
            src_ref=spec.at[me],
            dst_ref=spec.at[me],
            send_sem=spec_send.at[d],
            recv_sem=spec_recv.at[d],
            device_id={"sph": lax.rem(me + d, n_sph)},
            device_id_type=MESH,
        )
        copy.start()
        spec_copies.append(copy)

    for side in range(2):
        halo_copy(side).wait()
    around = split(
        jnp.concatenate(
            [
                halo[0].reshape(own * rows, block),
                coef_ref[pl.ds(first, own)].reshape(own * rows, block),
                halo[1].reshape(own * rows, block),
            ],
            axis=1,
        )
    )
    ids = lax.broadcasted_iota(jnp.int32, (3 * block, block), 0)
    start = (me - 1) * block
    for k in range(slots):
        chosen = jnp.where(ids == index_ref[k : k + 1, :] - start, 1.0, 0.0).astype(jnp.bfloat16)
        picked[k] = dot(around[0], chosen) + dot(around[1], chosen)

    for copy in spec_copies:
        copy.wait_recv()

    def spec_row(row):
        return spec[row // share, row % share : row % share + 1, :]

    for b in range(illums):
        real = [spec_row(b * 4 + q) for q in range(2)]
        imag = [spec_row(b * 4 + 2 + q) for q in range(2)]
        for p in range(2):
            r_real = [refl_ref[p * 2 + q : p * 2 + q + 1, :] for q in range(2)]
            r_imag = [refl_ref[4 + p * 2 + q : 5 + p * 2 + q, :] for q in range(2)]
            mirrored[b, p : p + 1, :] = sum(r_real[q] * real[q] - r_imag[q] * imag[q] for q in range(2))
            mirrored[b, 2 + p : 3 + p, :] = sum(r_real[q] * imag[q] + r_imag[q] * real[q] for q in range(2))

    up = (up_high[...], up_low[...])

    def respond(d):
        target = lax.rem(mine + d, n_wave) * own
        fields = []
        for i in range(own):
            rows_of = mirrored[target + i]
            real, imag = 0.0, 0.0
            for p in range(2):
                q_real, q_imag = proj_ref[0, p], proj_ref[1, p]
                m_real, m_imag = rows_of[p : p + 1], rows_of[2 + p : 3 + p]
                real = real + (q_real * m_real - q_imag * m_imag)
                imag = imag + (q_real * m_imag + q_imag * m_real)
            fields += [real, imag]
        products = dot3(split(jnp.concatenate(fields, axis=0)), up)
        for i in range(own):
            real = products[i * rows : i * rows + modes]
            imag = products[i * rows + modes : (i + 1) * rows]
            resp[d, i, :modes, :] = real[:, :block] - imag[:, block:]
            resp[d, i, modes:, :] = real[:, block:] + imag[:, :block]

    resp_copies = []
    for d in range(1, n_wave):
        respond(d)
        copy = pltpu.make_async_remote_copy(
            src_ref=resp.at[d],
            dst_ref=resp_in.at[d],
            send_sem=resp_send.at[d],
            recv_sem=resp_recv.at[d],
            device_id={"wave": lax.rem(mine + d, n_wave)},
            device_id_type=MESH,
        )
        copy.start()
        resp_copies.append(copy)
    respond(0)

    slot_ids = lax.broadcasted_iota(jnp.int32, (slots, block), 0)
    classes = jnp.where(slot_ids < count_ref[...], class_ref[...], -1)

    def fill(c, carry):
        binned = jnp.zeros((own * rows, block), jnp.float32)
        for k in range(slots):
            binned = binned + jnp.where(classes[k : k + 1, :] == c, picked[k], 0.0)
        high, low = split(binned)
        at = pl.ds(pl.multiple_of(c * rows, 16), rows)
        for i in range(own):
            bin_high[at, i * block : (i + 1) * block] = high[i * rows : (i + 1) * rows]
            bin_low[at, i * block : (i + 1) * block] = low[i * rows : (i + 1) * rows]
        return carry

    lax.fori_loop(0, offsets, fill, 0)
    translated = dot3(split(op_ref[...]), (bin_high[...], bin_low[...]))

    for copy in resp_copies:
        copy.wait_recv()
    exciting = []
    for i in range(own):
        value = inc_ref[first + i] + resp[0, i]
        for d in range(1, n_wave):
            value = value + resp_in[d, i]
        exciting.append(value + translated[:, i * block : (i + 1) * block])
    every = dot3(split(t_ref[...]), split(jnp.concatenate(exciting, axis=1)))
    for i in range(own):
        value = jnp.zeros((rows, block), jnp.float32)
        for t in range(types):
            value = value + jnp.where(
                type_ref[...] == t, every[t * rows : (t + 1) * rows, i * block : (i + 1) * block], 0.0
            )
        out_ref[first + i] = value

    out_copies = []
    for d in range(1, n_wave):
        copy = pltpu.make_async_remote_copy(
            src_ref=out_ref.at[pl.ds(first, own)],
            dst_ref=out_ref.at[pl.ds(first, own)],
            send_sem=out_send.at[d],
            recv_sem=out_recv.at[d],
            device_id={"wave": lax.rem(mine + d, n_wave)},
            device_id_type=MESH,
        )
        copy.start()
        out_copies.append(copy)
    for copy in part_copies + spec_copies + resp_copies:
        copy.wait_send()
    for copy in out_copies:
        copy.wait()


def per_device(
    n_sph, n_wave,
    coefficients, incident, positions, neighbour_index, link_class, link_count, sphere_type,
    translation, t_matrix, wave_grid, vertical, expansion, reflection, projector,
):
    illums, rows, block = coefficients.shape
    waves = vertical.shape[0]
    slots = neighbour_index.shape[0]
    offsets, types = translation.shape[1], t_matrix.shape[1]
    own = illums // n_wave
    share = illums * 4 // n_sph
    op_rows = jnp.transpose(realify(translation), (1, 0, 2)).reshape(rows, offsets * rows)
    t_rows = realify(t_matrix).reshape(types * rows, rows)
    args = (
        coefficients, incident, positions.T, neighbour_index, link_class, link_count.reshape(1, block),
        sphere_type.reshape(1, block), op_rows, t_rows, wave_grid, vertical.reshape(1, waves), expansion,
        reflection.reshape(8, waves), jnp.transpose(projector, (0, 2, 1, 3)),
    )
    f32, bf16 = jnp.float32, jnp.bfloat16
    sems = pltpu.SemaphoreType.DMA
    return pl.pallas_call(
        functools.partial(kernel, n_sph, n_wave, offsets, types),
        out_shape=jax.ShapeDtypeStruct(coefficients.shape, f32),
        in_specs=[pl.BlockSpec(memory_space=pltpu.VMEM)] * len(args),
        out_specs=pl.BlockSpec(memory_space=pltpu.VMEM),
        scratch_shapes=[
            pltpu.VMEM((2, own, rows, block), f32),
            pltpu.VMEM((n_sph, share, waves), f32),
            pltpu.VMEM((n_sph, share, waves), f32),
            pltpu.VMEM((n_sph, share, waves), f32),
            pltpu.VMEM((illums, 4, waves), f32),
            pltpu.VMEM((waves, 2 * block), bf16),
            pltpu.VMEM((waves, 2 * block), bf16),
            pltpu.VMEM((slots, own * rows, block), f32),
            pltpu.VMEM((offsets * rows, own * block), bf16),
            pltpu.VMEM((offsets * rows, own * block), bf16),
            pltpu.VMEM((n_wave, own, rows, block), f32),
            pltpu.VMEM((n_wave, own, rows, block), f32),
            sems((2,)), sems((2,)),
            sems((n_sph,)), sems((n_sph,)),
            sems((n_sph,)), sems((n_sph,)),
            sems((n_wave,)), sems((n_wave,)),
            sems((n_wave,)), sems((n_wave,)),
        ],
        compiler_params=pltpu.CompilerParams(
            collective_id=0, has_side_effects=True, vmem_limit_bytes=48 * 1024 * 1024
        ),
    )(*args)


def solution(mesh):
    placed = (
        P(None, None, "sph"),
        P(None, None, "sph"),
        P(None, "sph"),
        P(None, "sph"),
        P(None, "sph"),
        P("sph"),
        P("sph"),
        P(),
        P(),
        P(None, "wave"),
        P("wave"),
        P(None, None, None, "wave"),
        P(None, None, None, "wave"),
        P(None, None, None, "wave"),
    )
    return jax.shard_map(
        functools.partial(per_device, mesh.shape["sph"], mesh.shape["wave"]),
        mesh=mesh, in_specs=placed, out_specs=P(None, None, "sph"), check_vma=False,
    )
```

profile of v0, /device:TPU:0, one launch (start us, length us, event | category | flops | bytes accessed | tf_op | source)
XLA Modules:
  0.0 34.5 jit_solution(12760976877576465499)
XLA Ops:
  0.0 0.0 copy-start.9
  0.0 1.5 %slice_bitcast_fusion = (f32[26,48,48]{2,1,0:T(8,128)S(1)}, f32[26,48,48]{2,1,0:T(8,128)S(1)}) fusion(f32[2,26,48,48]{3,2,1,0:T(8,128)} %param.21), kind=kLoop, calls=%fused_computation.1 | loop fusion | bytes 958464 | tf_op jit(solution)/shard_map/squeeze | solution.py:18
  1.5 0.2 copy-done.9
  1.7 0.4 %maximum_bitcast_fusion = f32[96,26,96]{2,0,1:T(8,128)S(1)} fusion(f32[26,48,48]{2,1,0:T(8,128)S(1)} %get-tuple-element.6, f32[26,48,48]{2,1,0:T(8,128)S(1)} %get-tuple-element.5, f32[26,48,48]{2,1,0:T(8,128)S(1)} %fusion.1), kind=kLoop, calls=%fused_computation | loop fusion | flops 718848 | bytes 1677312 | tf_op jit(solution)/shard_map/transpose | solution.py:292
  2.1 0.4 %copy.19 = f32[96,26,96]{0,2,1:T(8,128)S(1)} copy(f32[96,26,96]{2,0,1:T(8,128)S(1)} %maximum_bitcast_fusion) | data formatting | bytes 1916928 | tf_op jit(solution)/shard_map/transpose | solution.py:292
  2.5 0.0 copy-start.10
  2.5 0.0 copy-start.11
  2.6 0.4 %copy.21.op_ref = f32[96,2496]{1,0:T(8,128)S(1)} copy(f32[96,2496]{0,1:T(8,128)S(1)} %bitcast.29) | data formatting | bytes 1916928 | tf_op jit(solution)/shard_map/reshape | solution.py:292
  3.0 0.5 %copy-done.10 = f32[2,4,48,48]{3,2,1,0:T(8,128)S(1)} copy-done((f32[2,4,48,48]{3,2,1,0:T(8,128)S(1)}, f32[2,4,48,48]{3,2,1,0:T(8,128)}, u32[]{:S(2)}) %copy-start.10) | copy-done | bytes 73752
  3.5 0.0 copy-start.13
  3.5 0.0 copy-start.12
  3.5 0.0 copy-start
  3.5 0.0 copy-start.1
  3.5 0.0 copy-start.2
  3.5 0.0 copy-start.3
  3.5 0.0 copy-start.4
  3.5 0.0 copy-start.5
  3.5 0.0 copy-start.6
  3.5 0.0 copy-start.7
  3.6 0.0 copy-start.8
  3.6 0.1 maximum_maximum_fusion
  3.7 0.0 copy-done.11
  3.7 0.1 copy.23
  3.8 0.4 %copy-done.13 = f32[3,128]{1,0:T(4,128)S(1)} copy-done((f32[3,128]{1,0:T(4,128)S(1)}, f32[3,128]{1,0:T(4,128)}, u32[]{:S(2)}) %copy-start.13) | copy-done | bytes 1560
  4.2 0.1 copy.18
  4.3 0.0 copy-done.12
  4.3 0.2 copy-done
  4.5 0.1 copy-done.1
  4.6 0.1 copy-done.2
  4.8 0.0 copy-done.3
  4.8 0.0 copy-done.4
  4.8 0.0 copy-done.5
  4.8 0.0 copy-done.6
  4.8 0.0 copy-done.7
  4.8 0.0 copy-done.8
  4.8 29.0 %shard_map.136 = f32[8,96,128]{2,1,0:T(8,128)S(1)} custom-call(f32[8,96,128]{2,1,0:T(8,128)S(1)} %copy-done, f32[8,96,128]{2,1,0:T(8,128)S(1)} %copy-done.1, f32[128,3]{1,0:T(8,128)S(1)} %bitcast.25, s32[12,128]{1,0:T(8,128)S(1)} %copy-done.3, s32[12,128]{1,0:T(8,128)S(1)} %copy-done.4, s32[1,128]{1,0:T(1,128)S(1)} %bitcast.27, s32[1,128]{1,0:T(1,128)S(1)} %bitcast.28, ...), custom_call_target="tpu_custom_call" | custom-call | tf_op jit(solution)/shard_map/pallas_call | solution.py:301
  33.8 0.7 %copy.25 = f32[8,96,128]{2,1,0:T(8,128)} copy(f32[8,96,128]{2,1,0:T(8,128)S(1)} %shard_map.136) | data formatting | bytes 786432
  (4 shorter events, 0.1 us)
Async XLA Ops:
  0.0 1.7 %copy-start.9 = (f32[2,26,48,48]{3,2,1,0:T(8,128)S(1)}, f32[2,26,48,48]{3,2,1,0:T(8,128)}, u32[]{:S(2)}) copy-start(f32[2,26,48,48]{3,2,1,0:T(8,128)} %param.21) | copy-start | bytes 1437700
  2.5 0.9 %copy-start.10 = (f32[2,4,48,48]{3,2,1,0:T(8,128)S(1)}, f32[2,4,48,48]{3,2,1,0:T(8,128)}, u32[]{:S(2)}) copy-start(f32[2,4,48,48]{3,2,1,0:T(8,128)} %param.22) | copy-start | bytes 221188
  2.5 1.2 %copy-start.11 = (f32[2,48,2,512]{3,2,1,0:T(2,128)S(1)}, f32[2,48,2,512]{3,2,1,0:T(2,128)}, u32[]{:S(2)}) copy-start(f32[2,48,2,512]{3,2,1,0:T(2,128)} %param.27) | copy-start | bytes 1179652
  3.5 0.7 %copy-start.13 = (f32[3,128]{1,0:T(4,128)S(1)}, f32[3,128]{1,0:T(4,128)}, u32[]{:S(2)}) copy-start(f32[3,128]{1,0:T(4,128)} %param.16) | copy-start | bytes 4612
  3.5 0.8 %copy-start.12 = (f32[2,2,2,512]{3,2,1,0:T(2,128)S(1)}, f32[2,2,2,512]{3,2,1,0:T(2,128)}, u32[]{:S(2)}) copy-start(f32[2,2,2,512]{3,2,1,0:T(2,128)} %param.26) | copy-start | bytes 49156
  3.5 1.1 %copy-start = (f32[8,96,128]{2,1,0:T(8,128)S(1)}, f32[8,96,128]{2,1,0:T(8,128)}, u32[]{:S(2)}) copy-start(f32[8,96,128]{2,1,0:T(8,128)} %coef_ref.1) | copy-start | bytes 1179652
  3.5 1.2 %copy-start.1 = (f32[8,96,128]{2,1,0:T(8,128)S(1)}, f32[8,96,128]{2,1,0:T(8,128)}, u32[]{:S(2)}) copy-start(f32[8,96,128]{2,1,0:T(8,128)} %inc_ref.1) | copy-start | bytes 1179652
  3.5 1.3 %copy-start.2 = (f32[2,2,48,512]{3,2,1,0:T(8,128)S(1)}, f32[2,2,48,512]{3,2,1,0:T(8,128)}, u32[]{:S(2)}) copy-start(f32[2,2,48,512]{3,2,1,0:T(8,128)} %exp_ref.1) | copy-start | bytes 1179652
  3.5 1.3 %copy-start.3 = (s32[12,128]{1,0:T(8,128)S(1)}, s32[12,128]{1,0:T(8,128)}, u32[]{:S(2)}) copy-start(s32[12,128]{1,0:T(8,128)} %index_ref.1) | copy-start | bytes 18436
  3.5 1.3 %copy-start.4 = (s32[12,128]{1,0:T(8,128)S(1)}, s32[12,128]{1,0:T(8,128)}, u32[]{:S(2)}) copy-start(s32[12,128]{1,0:T(8,128)} %class_ref.1) | copy-start | bytes 18436
  3.5 1.3 %copy-start.5 = (s32[2,512]{1,0:T(2,128)S(1)}, s32[2,512]{1,0:T(2,128)}, u32[]{:S(2)}) copy-start(s32[2,512]{1,0:T(2,128)} %grid_ref.1) | copy-start | bytes 12292
  3.5 1.2 %copy-start.6 = (f32[512]{0:T(512)S(1)}, f32[512]{0:T(512)}, u32[]{:S(2)}) copy-start(f32[512]{0:T(512)} %param.24) | copy-start | bytes 6148
  3.5 1.2 %copy-start.7 = (s32[128]{0:T(128)S(1)}, s32[128]{0:T(128)}, u32[]{:S(2)}) copy-start(s32[128]{0:T(128)} %param.19) | copy-start | bytes 1540
  3.6 1.2 %copy-start.8 = (s32[128]{0:T(128)S(1)}, s32[128]{0:T(128)}, u32[]{:S(2)}) copy-start(s32[128]{0:T(128)} %param.20) | copy-start | bytes 1540
where the time goes:
time: 34.7 us; the launch traced here: 34.5 us
  Pallas kernels  29 us (84%)
  local copies, waits for them, and re-layouts  4.8 us (14%)
  other arithmetic  0.57 us (2%)
    pallas_call x1, Pallas kernels, per_device(): pl.pallas_call(functools.partial(kernel, n_sph, n_wave, offsets, types),...  29 us
    unnamed x31, local copies, waits for them, and re-layouts  2.53 us
    squeeze x2, local copies, waits for them, and re-layouts, realify(): upper_half = jnp.concatenate([complex_pair[0], -complex_pair[1]], axis=-1)  1.47 us

commit v1 on v0

--- a/solution.py
+++ b/solution.py
@@ -14,9 +14,9 @@
 COS_TERMS = [(-1) ** k * math.pi ** (2 * k) / math.factorial(2 * k) for k in range(7)]
 
 
-def realify(complex_pair):
-    upper_half = jnp.concatenate([complex_pair[0], -complex_pair[1]], axis=-1)
-    lower_half = jnp.concatenate([complex_pair[1], complex_pair[0]], axis=-1)
+def realify(real, imag):
+    upper_half = jnp.concatenate([real, -imag], axis=-1)
+    lower_half = jnp.concatenate([imag, real], axis=-1)
     return jnp.concatenate([upper_half, lower_half], axis=-2)
 
 
@@ -49,14 +49,33 @@
 
 
 def kernel(
-    n_sph, n_wave, offsets, types,
-    coef_ref, inc_ref, pos_ref, index_ref, class_ref, count_ref, type_ref, op_ref, t_ref,
-    grid_ref, vert_ref, exp_ref, refl_ref, proj_ref,
-    out_ref,
-    halo, part, part_in, spec, mirrored, up_high, up_low, picked, bin_high, bin_low, resp, resp_in,
+    n_sph, n_wave, n_args, *refs
+):
+    given, out_ref, here, load_sem = (
+        refs[:n_args], refs[n_args], refs[n_args + 1 : 2 * n_args + 1], refs[2 * n_args + 1]
+    )
+    body(n_sph, n_wave, given, here, load_sem, out_ref, *refs[2 * n_args + 2 :])
+
+
+def body(
+    n_sph, n_wave, given, here, load_sem, out_ref,
+    halo, part, part_in, spec, mirrored, up_high, up_low, picked, bin_high, bin_low, op_high, op_low, proj, resp, resp_in,
     halo_send, halo_recv, part_send, part_recv, spec_send, spec_recv,
     resp_send, resp_recv, out_send, out_recv,
 ):
+    (
+        coef_ref, pos_ref, grid_ref, vert_ref, exp_ref, index_ref, class_ref, count_ref, type_ref,
+        refl_ref, proj_ref, op_ref, t_ref, inc_ref,
+    ) = here
+    loads = {}
+    for n, (source, target) in enumerate(zip(given, here)):
+        loads[id(target)] = pltpu.make_async_copy(source, target, load_sem.at[n])
+        loads[id(target)].start()
+
+    def ready(*names):
+        for name in names:
+            loads[id(name)].wait()
+
     me = lax.axis_index("sph")
     mine = lax.axis_index("wave")
     illums, rows, block = coef_ref.shape
@@ -64,6 +83,7 @@
     waves = vert_ref.shape[1]
     slots = index_ref.shape[0]
     own = illums // n_wave
+    offsets, types = op_ref.shape[1], t_ref.shape[1]
     first = mine * own
     share = part.shape[1]
 
@@ -77,7 +97,7 @@
     def halo_copy(side):
         step = 1 if side == 0 else n_sph - 1
         return pltpu.make_async_remote_copy(
-            src_ref=coef_ref.at[pl.ds(first, own)],
+            src_ref=given[0].at[pl.ds(first, own)],
             dst_ref=halo.at[side],
             send_sem=halo_send.at[side],
             recv_sem=halo_recv.at[side],
@@ -88,12 +108,17 @@
     for side in range(2):
         halo_copy(side).start()
 
+    ready(coef_ref, pos_ref, grid_ref, vert_ref, exp_ref)
+    centres = jnp.concatenate(
+        [pos_ref[...], jnp.zeros((block - pos_ref.shape[0], block), jnp.float32)], axis=0
+    ).T
+
     def angles(w):
         wave = slice(w * LANES, (w + 1) * LANES)
         across = grid_ref[0:1, wave].astype(jnp.float32)
         along = grid_ref[1:2, wave].astype(jnp.float32)
-        plane = pos_ref[:, 0:1] * across + pos_ref[:, 1:2] * along
-        height = pos_ref[:, 2:3] * (vert_ref[:, wave] * (0.5 / math.pi))
+        plane = centres[:, 0:1] * across + centres[:, 1:2] * along
+        height = centres[:, 2:3] * (vert_ref[:, wave] * (0.5 / math.pi))
         return plane - jnp.floor(plane + 0.5), height
 
     coef = split(coef_ref[...].reshape(illums * rows, block))
@@ -138,6 +163,21 @@
         up_high[wave, :] = high
         up_low[wave, :] = low
 
+    ready(proj_ref, op_ref)
+    for c in range(2):
+        for p in range(2):
+            proj[c, p] = proj_ref[c, :, p, :]
+    blank = jnp.zeros((rows, LANES - rows), jnp.float32)
+
+    def widen(c, carry):
+        high, low = split(jnp.concatenate([realify(op_ref[0, c], op_ref[1, c]), blank], axis=1))
+        at = pl.ds(pl.multiple_of(c * LANES, LANES), LANES)
+        op_high[:, at] = high
+        op_low[:, at] = low
+        return carry
+
+    lax.fori_loop(0, offsets, widen, 0)
+
     total = part[me]
     for d, copy in enumerate(part_copies, 1):
         copy.wait_recv()
@@ -157,6 +197,7 @@
         copy.start()
         spec_copies.append(copy)
 
+    ready(index_ref, class_ref, count_ref, type_ref, refl_ref, t_ref, inc_ref)
     for side in range(2):
         halo_copy(side).wait()
     around = split(
@@ -175,6 +216,24 @@
         chosen = jnp.where(ids == index_ref[k : k + 1, :] - start, 1.0, 0.0).astype(jnp.bfloat16)
         picked[k] = dot(around[0], chosen) + dot(around[1], chosen)
 
+    slot_ids = lax.broadcasted_iota(jnp.int32, (slots, block), 0)
+    classes = jnp.where(slot_ids < count_ref[...], class_ref[...], -1)
+
+    def fill(c, carry):
+        binned = jnp.zeros((own * rows, block), jnp.float32)
+        for k in range(slots):
+            binned = binned + jnp.where(classes[k : k + 1, :] == c, picked[k], 0.0)
+        high, low = split(binned)
+        at = pl.ds(pl.multiple_of(c * LANES, LANES), rows)
+        rest = pl.ds(pl.multiple_of(c * LANES + rows, 16), LANES - rows)
+        for i in range(own):
+            bin_high[at, i * block : (i + 1) * block] = high[i * rows : (i + 1) * rows]
+            bin_low[at, i * block : (i + 1) * block] = low[i * rows : (i + 1) * rows]
+        for bins in (bin_high, bin_low):
+            bins[rest, :] = jnp.zeros((LANES - rows, own * block), jnp.bfloat16)
+        return carry
+
+    lax.fori_loop(0, offsets, fill, 0)
     for copy in spec_copies:
         copy.wait_recv()
 
@@ -185,8 +244,8 @@
         real = [spec_row(b * 4 + q) for q in range(2)]
         imag = [spec_row(b * 4 + 2 + q) for q in range(2)]
         for p in range(2):
-            r_real = [refl_ref[p * 2 + q : p * 2 + q + 1, :] for q in range(2)]
-            r_imag = [refl_ref[4 + p * 2 + q : 5 + p * 2 + q, :] for q in range(2)]
+            r_real = [refl_ref[0, p, q : q + 1, :] for q in range(2)]
+            r_imag = [refl_ref[1, p, q : q + 1, :] for q in range(2)]
             mirrored[b, p : p + 1, :] = sum(r_real[q] * real[q] - r_imag[q] * imag[q] for q in range(2))
             mirrored[b, 2 + p : 3 + p, :] = sum(r_real[q] * imag[q] + r_imag[q] * real[q] for q in range(2))
 
@@ -199,7 +258,7 @@
             rows_of = mirrored[target + i]
             real, imag = 0.0, 0.0
             for p in range(2):
-                q_real, q_imag = proj_ref[0, p], proj_ref[1, p]
+                q_real, q_imag = proj[0, p], proj[1, p]
                 m_real, m_imag = rows_of[p : p + 1], rows_of[2 + p : 3 + p]
                 real = real + (q_real * m_real - q_imag * m_imag)
                 imag = imag + (q_real * m_imag + q_imag * m_real)
@@ -214,64 +273,47 @@
     resp_copies = []
     for d in range(1, n_wave):
         respond(d)
-        copy = pltpu.make_async_remote_copy(
-            src_ref=resp.at[d],
-            dst_ref=resp_in.at[d],
-            send_sem=resp_send.at[d],
-            recv_sem=resp_recv.at[d],
-            device_id={"wave": lax.rem(mine + d, n_wave)},
-            device_id_type=MESH,
-        )
-        copy.start()
-        resp_copies.append(copy)
+        for i in range(own):
+            copy = pltpu.make_async_remote_copy(
+                src_ref=resp.at[d, i],
+                dst_ref=resp_in.at[d, i],
+                send_sem=resp_send.at[d, i],
+                recv_sem=resp_recv.at[d, i],
+                device_id={"wave": lax.rem(mine + d, n_wave)},
+                device_id_type=MESH,
+            )
+            copy.start()
+            resp_copies.append(copy)
     respond(0)
 
-    slot_ids = lax.broadcasted_iota(jnp.int32, (slots, block), 0)
-    classes = jnp.where(slot_ids < count_ref[...], class_ref[...], -1)
-
-    def fill(c, carry):
-        binned = jnp.zeros((own * rows, block), jnp.float32)
-        for k in range(slots):
-            binned = binned + jnp.where(classes[k : k + 1, :] == c, picked[k], 0.0)
-        high, low = split(binned)
-        at = pl.ds(pl.multiple_of(c * rows, 16), rows)
-        for i in range(own):
-            bin_high[at, i * block : (i + 1) * block] = high[i * rows : (i + 1) * rows]
-            bin_low[at, i * block : (i + 1) * block] = low[i * rows : (i + 1) * rows]
-        return carry
-
-    lax.fori_loop(0, offsets, fill, 0)
-    translated = dot3(split(op_ref[...]), (bin_high[...], bin_low[...]))
-
-    for copy in resp_copies:
-        copy.wait_recv()
-    exciting = []
+    translated = dot3((op_high[...], op_low[...]), (bin_high[...], bin_low[...]))
+
+    t_rows = split(
+        jnp.concatenate([realify(t_ref[0, t], t_ref[1, t]) for t in range(types)], axis=0)
+    )
+    out_copies = []
     for i in range(own):
-        value = inc_ref[first + i] + resp[0, i]
+        value = inc_ref[first + i] + resp[0, i] + translated[:, i * block : (i + 1) * block]
+        for copy in resp_copies[i::own]:
+            copy.wait_recv()
         for d in range(1, n_wave):
             value = value + resp_in[d, i]
-        exciting.append(value + translated[:, i * block : (i + 1) * block])
-    every = dot3(split(t_ref[...]), split(jnp.concatenate(exciting, axis=1)))
-    for i in range(own):
+        every = dot3(t_rows, split(value))
         value = jnp.zeros((rows, block), jnp.float32)
         for t in range(types):
-            value = value + jnp.where(
-                type_ref[...] == t, every[t * rows : (t + 1) * rows, i * block : (i + 1) * block], 0.0
+            value = value + jnp.where(type_ref[...] == t, every[t * rows : (t + 1) * rows], 0.0)
+        out_ref[first + i] = value
+        for d in range(1, n_wave):
+            copy = pltpu.make_async_remote_copy(
+                src_ref=out_ref.at[first + i],
+                dst_ref=out_ref.at[first + i],
+                send_sem=out_send.at[d, i],
+                recv_sem=out_recv.at[d, i],
+                device_id={"wave": lax.rem(mine + d, n_wave)},
+                device_id_type=MESH,
             )
-        out_ref[first + i] = value
-
-    out_copies = []
-    for d in range(1, n_wave):
-        copy = pltpu.make_async_remote_copy(
-            src_ref=out_ref.at[pl.ds(first, own)],
-            dst_ref=out_ref.at[pl.ds(first, own)],
-            send_sem=out_send.at[d],
-            recv_sem=out_recv.at[d],
-            device_id={"wave": lax.rem(mine + d, n_wave)},
-            device_id_type=MESH,
-        )
-        copy.start()
-        out_copies.append(copy)
+            copy.start()
+            out_copies.append(copy)
     for copy in part_copies + spec_copies + resp_copies:
         copy.wait_send()
     for copy in out_copies:
@@ -286,24 +328,23 @@
     illums, rows, block = coefficients.shape
     waves = vertical.shape[0]
     slots = neighbour_index.shape[0]
-    offsets, types = translation.shape[1], t_matrix.shape[1]
+    offsets = translation.shape[1]
     own = illums // n_wave
     share = illums * 4 // n_sph
-    op_rows = jnp.transpose(realify(translation), (1, 0, 2)).reshape(rows, offsets * rows)
-    t_rows = realify(t_matrix).reshape(types * rows, rows)
     args = (
-        coefficients, incident, positions.T, neighbour_index, link_class, link_count.reshape(1, block),
-        sphere_type.reshape(1, block), op_rows, t_rows, wave_grid, vertical.reshape(1, waves), expansion,
-        reflection.reshape(8, waves), jnp.transpose(projector, (0, 2, 1, 3)),
+        coefficients, positions, wave_grid, vertical.reshape(1, waves), expansion, neighbour_index, link_class,
+        link_count.reshape(1, block), sphere_type.reshape(1, block), reflection, projector, translation, t_matrix,
+        incident,
     )
     f32, bf16 = jnp.float32, jnp.bfloat16
     sems = pltpu.SemaphoreType.DMA
     return pl.pallas_call(
-        functools.partial(kernel, n_sph, n_wave, offsets, types),
+        functools.partial(kernel, n_sph, n_wave, len(args)),
         out_shape=jax.ShapeDtypeStruct(coefficients.shape, f32),
-        in_specs=[pl.BlockSpec(memory_space=pltpu.VMEM)] * len(args),
+        in_specs=[pl.BlockSpec(memory_space=pltpu.HBM)] * len(args),
         out_specs=pl.BlockSpec(memory_space=pltpu.VMEM),
-        scratch_shapes=[
+        scratch_shapes=[pltpu.VMEM(a.shape, a.dtype) for a in args] + [
+            sems((len(args),)),
             pltpu.VMEM((2, own, rows, block), f32),
             pltpu.VMEM((n_sph, share, waves), f32),
             pltpu.VMEM((n_sph, share, waves), f32),
@@ -312,18 +353,21 @@
             pltpu.VMEM((waves, 2 * block), bf16),
             pltpu.VMEM((waves, 2 * block), bf16),
             pltpu.VMEM((slots, own * rows, block), f32),
-            pltpu.VMEM((offsets * rows, own * block), bf16),
-            pltpu.VMEM((offsets * rows, own * block), bf16),
+            pltpu.VMEM((offsets * LANES, own * block), bf16),
+            pltpu.VMEM((offsets * LANES, own * block), bf16),
+            pltpu.VMEM((rows, offsets * LANES), bf16),
+            pltpu.VMEM((rows, offsets * LANES), bf16),
+            pltpu.VMEM((2, 2, rows // 2, waves), f32),
             pltpu.VMEM((n_wave, own, rows, block), f32),
             pltpu.VMEM((n_wave, own, rows, block), f32),
             sems((2,)), sems((2,)),
             sems((n_sph,)), sems((n_sph,)),
             sems((n_sph,)), sems((n_sph,)),
-            sems((n_wave,)), sems((n_wave,)),
-            sems((n_wave,)), sems((n_wave,)),
+            sems((n_wave, own)), sems((n_wave, own)),
+            sems((n_wave, own)), sems((n_wave, own)),
         ],
         compiler_params=pltpu.CompilerParams(
-            collective_id=0, has_side_effects=True, vmem_limit_bytes=48 * 1024 * 1024
+            collective_id=0, has_side_effects=True, vmem_limit_bytes=60 * 1024 * 1024
         ),
     )(*args)
 

time: 34.7 us -> 31 us (0.89)
  local copies, waits for them, and re-layouts: 4.8 us -> 1.77 us
  other arithmetic: 0.57 us -> 0 us
    squeeze x2 -> x0, local copies, waits for them, and re-layouts: 1.47 us -> none  [realify(): upper_half = jnp.concatenate([complex_pair[0], -complex_pair[1]], axis=-1)]
    unnamed x31 -> x1, local copies, waits for them, and re-layouts: 2.53 us -> 1.77 us
    reshape x2 -> x0, local copies, waits for them, and re-layouts: 0.41 us -> none  [the longest x1 0.39 us: per_device(): jnp.transpose(realify(translation), (1, 0, 2)).reshape(rows, offsets * rows)]
    transpose x1 -> x0, other arithmetic: 0.4 us -> none  [per_device(): jnp.transpose(realify(translation), (1, 0, 2)).reshape(rows, offsets * rows)]
    transpose x1 -> x0, local copies, waits for them, and re-layouts: 0.39 us -> none  [per_device(): jnp.transpose(realify(translation), (1, 0, 2)).reshape(rows, offsets * rows)]
where the time goes in v1:
time: 31 us; the launch traced here: 30.9 us
  Pallas kernels  29.1 us (94%)
  local copies, waits for them, and re-layouts  1.77 us (6%)
    pallas_call x1, Pallas kernels, per_device(): pl.pallas_call(functools.partial(kernel, n_sph, n_wave, len(args)), out_s...  29.1 us
    unnamed x1, local copies, waits for them, and re-layouts  1.77 us

profile of v1, /device:TPU:0, one launch (start us, length us, event | category | flops | bytes accessed | tf_op | source)
XLA Modules:
  0.0 30.9 jit_solution(11216408296896848199)
XLA Ops:
  0.0 29.1 %shard_map.136 = f32[8,96,128]{2,1,0:T(8,128)} custom-call(f32[8,96,128]{2,1,0:T(8,128)} %refs_0_.1, f32[3,128]{1,0:T(4,128)} %refs_1_.1, s32[2,512]{1,0:T(2,128)} %refs_2_.1, f32[1,512]{1,0:T(1,128)} %bitcast.3, f32[2,2,48,512]{3,2,1,0:T(8,128)} %refs_4_.1, s32[12,128]{1,0:T(8,128)} %refs_5_.1, s32[12,128]{1,0:T(8,128)} %refs_6_.1, s32[1,128]{1,0:T(1,128)} %bitcast.4, ...), custom_call_target="tpu_custom_call" | custom-call | tf_op jit(solution)/shard_map/pallas_call | solution.py:341
  29.1 1.8 %copy.16 = f32[8,96,128]{2,1,0:T(8,128)} copy(f32[8,96,128]{2,1,0:T(8,128)} %shard_map.136) | data formatting | bytes 786432
